TPU v7x, 256 devices: a whole 4x4x8 slice. The times are simulated.
256 devices in a mesh: lang: 8 (over x, core), dp: 32 (over z, y).
Axes of the slice: x: 4, y: 4, z: 8, core: 2. Of those that a mesh axis runs over, the one named last changes fastest.
Arguments:
- src_emb: bfloat16 [32768, 768], P(('lang', 'dp')), may hold values from -6 to 6
- tgt_emb: bfloat16 [8, 4096, 768], P(None, ('lang', 'dp')), may hold values from -6 to 6
- slot_group: int32 [8], replicated, may hold values from 0 to 7, each once
- counts: int32 [8], replicated, may hold values from 1024 to 4096, as said below
- align: int32 [8, 4096], P('lang'), may hold values from 0 to 4095, each once within a row
- pair_weight: float32 [8], replicated, may hold values from 4 to 40
Outputs:
- grad_src: bfloat16 [32768, 768], P(('lang', 'dp'))
- grad_tgt: bfloat16 [8, 4096, 768], P(None, ('lang', 'dp'))
- pair_loss: float32 [8], P('lang')
Inputs may be any that keep to these rules, and one draw needn't show every extreme that they name: `counts`: at least one pair has all 4096 sentences live. `align`: each row is a permutation.
All inputs are finite; a program needn't handle non-finite values.
Results may differ from a plain program's by a relative error of at most 0.0057.
Values may be sent and summed in bfloat16 or wider, within the bound.
A program may use at most 64 MiB of HBM per device.

v0:
```python
import math
import jax
import jax.numpy as jnp
from jax import lax
from jax.sharding import PartitionSpec as P

MARGIN = 0.3
LOW_FILL = -1e30


def combined_all(value, axis, combine):
    everything = jax.tree.map(lambda part: lax.all_gather(part, axis), value)
    initial = jax.tree.map(lambda part: part[0], everything)

    def lap(k, so_far):
        return combine(so_far, jax.tree.map(lambda part: part[k], everything))

    return lax.fori_loop(1, lax.axis_size(axis), lap, initial)


def target_index(offset, col_count, row_count, per_slot, data_size):
    position = offset + jnp.arange(col_count, dtype=jnp.int32)
    source = position // row_count
    within = position % row_count
    return (within // per_slot * data_size + source) * per_slot + within % per_slot


def tile_scores(
    src_rows, tile_rows, offset, my_align, col_live_global, per_slot, data_size, inv_root
):
    row_count = src_rows.shape[0]
    tgt_index = target_index(offset, tile_rows.shape[0], row_count, per_slot, data_size)
    raw_dot = lax.dot_general(
        src_rows, tile_rows, (((1,), (1,)), ((), ())), preferred_element_type=jnp.float32
    )
    is_pos = tgt_index[None, :] == my_align[:, None]
    scores_f = raw_dot * inv_root - MARGIN * is_pos.astype(jnp.float32)
    col_ok = col_live_global[tgt_index] > 0.5
    return (scores_f, is_pos, col_ok)


def row_update(old_max, scores_f, col_ok):
    masked = jnp.where(col_ok[None, :], scores_f, LOW_FILL)
    new_max = jnp.maximum(old_max, jnp.max(masked, axis=1))
    fresh = jnp.sum(jnp.where(col_ok[None, :], jnp.exp(scores_f - new_max[:, None]), 0.0), axis=1)
    return (new_max, fresh)


def column_stats(scores_f, row_live):
    col_max = jnp.max(jnp.where(row_live[:, None], scores_f, LOW_FILL), axis=0)
    col_sum = jnp.sum(
        jnp.where(row_live[:, None], jnp.exp(scores_f - col_max[None, :]), 0.0), axis=0
    )
    return (col_max, col_sum)


def grad_block(scores_f, is_pos, col_ok, row_lse, col_lse_all, row_live, weight):
    both_live = row_live[:, None] & col_ok[None, :]
    by_row = jnp.where(both_live, jnp.exp(scores_f - row_lse[:, None]), 0.0)
    by_col = jnp.where(both_live, jnp.exp(scores_f - col_lse_all[None, :]), 0.0)
    pos_hit = (is_pos & row_live[:, None]).astype(jnp.float32)
    return (weight * (by_row + by_col - 2.0 * pos_hit)).astype(jnp.bfloat16)


def merge_columns(first_part, second_part):
    top_val = jnp.maximum(first_part[0], second_part[0])
    summed = first_part[1] * jnp.exp(first_part[0] - top_val) + second_part[1] * jnp.exp(
        second_part[0] - top_val
    )
    return (top_val, summed)


def per_device(src_emb, tgt_emb, slot_group, counts, align, pair_weight):
    lang_size = lax.axis_size("lang")
    data_size = lax.axis_size("dp")
    row_count, emb_width = src_emb.shape
    per_slot = tgt_emb.shape[1]
    pair_rows = row_count * data_size
    inv_root = 1.0 / math.sqrt(emb_width)
    group_index = lax.axis_index("lang")
    shard_index = lax.axis_index("dp")
    slot_ids = jnp.arange(lang_size, dtype=jnp.int32)
    slot_of_group = jnp.zeros((lang_size,), jnp.int32).at[slot_group].set(slot_ids)
    ordered = tgt_emb[slot_of_group]
    arrived = lax.all_to_all(ordered, "lang", split_axis=0, concat_axis=1, tiled=True)
    partner = arrived[0]
    live_count = counts[group_index]
    weight = pair_weight[group_index]
    pair_align = align[0]
    all_rows = jnp.arange(pair_rows, dtype=jnp.int32)
    col_live_global = (
        jnp.zeros((pair_rows,), jnp.float32)
        .at[pair_align]
        .set((all_rows < live_count).astype(jnp.float32))
    )
    my_rows = shard_index * row_count + jnp.arange(row_count, dtype=jnp.int32)
    row_live = my_rows < live_count
    my_align = lax.dynamic_slice_in_dim(pair_align, shard_index * row_count, row_count)
    gathered_index = target_index(0, pair_rows, row_count, per_slot, data_size)
    col_live_gathered = col_live_global[gathered_index]
    start_max = jnp.full((row_count,), LOW_FILL, jnp.float32)
    all_targets = lax.all_gather(partner, "dp", axis=0, tiled=True)
    scores_f, is_pos, col_ok = tile_scores(
        src_emb, all_targets, 0, my_align, col_live_global, per_slot, data_size, inv_root
    )
    row_max, row_sum = row_update(start_max, scores_f, col_ok)
    col_max, col_sum = column_stats(scores_f, row_live)
    pos_score = jnp.sum(jnp.where(is_pos, scores_f, 0.0), axis=1)
    merged_max, merged_sum = combined_all((col_max, col_sum), "dp", merge_columns)
    col_lse_all = merged_max + jnp.log(merged_sum + (1.0 - col_live_gathered))
    col_lse_global = jnp.zeros((pair_rows,), jnp.float32).at[gathered_index].set(col_lse_all)
    row_lse = row_max + jnp.log(row_sum + (1.0 - row_live.astype(jnp.float32)))
    terms = jnp.where(row_live, row_lse + col_lse_global[my_align] - 2.0 * pos_score, 0.0)
    loss_total = lax.psum(jnp.sum(terms), "dp")
    pair_loss = (loss_total / live_count.astype(jnp.float32)).reshape(1)
    grad_tile = grad_block(scores_f, is_pos, col_ok, row_lse, col_lse_all, row_live, weight)
    grad_rows = jnp.dot(grad_tile, all_targets, preferred_element_type=jnp.float32)
    own_terms = lax.psum_scatter(
        lax.dot_general(
            grad_tile, src_emb, (((0,), (0,)), ((), ())), preferred_element_type=jnp.float32
        ),
        "dp",
        scatter_dimension=0,
        tiled=True,
    )
    grad_src = (grad_rows * inv_root).astype(jnp.bfloat16)
    grad_local = (own_terms * inv_root).astype(jnp.bfloat16)
    returned = lax.all_to_all(
        grad_local.reshape(1, row_count, emb_width), "lang", split_axis=1, concat_axis=0, tiled=True
    )
    grad_tgt = returned[slot_group]
    return (grad_src, grad_tgt, pair_loss)


def solution(mesh):
    in_specs = (
        P(("lang", "dp"), None),
        P(None, ("lang", "dp"), None),
        P(),
        P(),
        P("lang", None),
        P(),
    )
    out_specs = (P(("lang", "dp"), None), P(None, ("lang", "dp"), None), P("lang"))
    return jax.shard_map(
        per_device, mesh=mesh, in_specs=in_specs, out_specs=out_specs, check_vma=False
    )
```

profile of v0, /device:TPU:2, one launch (start us, length us, event | category | flops | bytes accessed | tf_op | source)
XLA Modules:
  0.0 611.2 jit_solution(6739788015881884098)
XLA Ops:
  7.2 0.7 compare_select_fusion.9
  7.9 0.6 scatter_custom_fusion.1
  8.6 1.5 gather_fusion.1
  10.0 10.7 %all_to_all.21 = bf16[8,16,768]{2,1,0:T(8,128)(2,1)} all-to-all(bf16[8,16,768]{2,1,0:T(8,128)(2,1)S(1)} %gather_fusion.1), channel_id=1, replica_groups=mesh['lang'=8,'dp'=32] {'lang'}, dimensions={0} | all-to-all | bytes 393216 | tf_op jit(solution)/shard_map/all_to_all | solution.py:85
  20.8 1.2 dynamic_slice.32
  22.1 1.3 dynamic_slice.31
  23.4 0.6 fusion.29
  24.1 0.7 compare_select_fusion.3
  24.8 15.5 %scatter_custom_fusion = f32[4096]{0:T(1024)S(1)} fusion(s32[4096]{0:T(1024)S(1)} %bitcast.43, f32[4096]{0:T(1024)S(1)} %fusion.29, f32[]{:T(128)} %constant.134.clone.1), kind=kCustom, calls=%fused_computation.80 | custom fusion | bytes 16388 | tf_op jit(solution)/shard_map/scatter | solution.py:94
  40.4 23.0 %gather_fusion = f32[4096]{0:T(1024)S(1)} fusion(f32[4096]{0:T(1024)S(1)} %scatter_custom_fusion, s32[4096]{0:T(1024)S(1)} %broadcast_clamp_fusion), kind=kCustom, calls=%fused_computation | custom fusion | bytes 49152 | tf_op jit(solution)/shard_map/gather | solution.py:38
  63.5 0.7 add_compare_fusion
  64.1 0.7 fusion.38
  64.8 0.7 fusion.35
  65.5 45.6 %all-gather.4.cloned.1.call-done = bf16[4096,768]{1,0:T(8,128)(2,1)} async-done(((bf16[128,768]{1,0:T(8,128)(2,1)}), bf16[4096,768]{1,0:T(8,128)(2,1)}) %all-gather.4.cloned.1.call-update) | async-done | bytes 6291472 | tf_op jit(solution)/shard_map/all_gather | solution.py:102
  111.1 4.9 select_reduce_fusion.3
  116.0 48.0 %all-gather = f32[131072]{0:T(1024)S(1)} all-gather(f32[4096]{0:T(1024)S(1)} %get-tuple-element.142), channel_id=2, replica_groups=mesh['lang'=8,'dp'=32] {'dp'}, dimensions={0}, use_global_device_ids=true | all-gather | bytes 540672 | tf_op jit(solution)/shard_map/all_gather | solution.py:12
  164.2 4.1 fusion.6
  168.3 47.5 %all-gather.1 = f32[131072]{0:T(1024)S(1)} all-gather(f32[4096]{0:T(1024)S(1)} %get-tuple-element.139), channel_id=3, replica_groups=mesh['lang'=8,'dp'=32] {'dp'}, dimensions={0}, use_global_device_ids=true | all-gather | bytes 540672 | tf_op jit(solution)/shard_map/all_gather | solution.py:12
  215.7 0.9 reshape.345
  216.6 30.5 %while.17 = (s32[]{:T(128)}, f32[4096]{0:T(1024)S(1)}, f32[4096]{0:T(1024)S(1)}, f32[32,4096]{1,0:T(8,128)S(1)}, f32[32,4096]{1,0:T(8,128)}, /*index=5*/s32[]{:T(128)}, s32[]{:T(128)}, s32[]{:T(128)}) while((s32[]{:T(128)}, f32[4096]{0:T(1024)S(1)}, f32[4096]{0:T(1024)S(1)}, f32[32,4096]{1,0:T(8,128)S(1)}, f32[32,4096]{1,0:T(8,128)}, ...), condition=%wide.region_7.8_spmd, body=%wide.region_6.7_spmd.sunk | while | flops 24581 | bytes 163971 | solution.py:18
  216.6 0.9 constant_dynamic-slice_fusion.4
  217.6 0.9 constant_dynamic-slice_fusion.4
  218.6 0.9 constant_dynamic-slice_fusion.4
  219.5 0.9 constant_dynamic-slice_fusion.4
  220.5 0.9 constant_dynamic-slice_fusion.4
  221.5 0.9 constant_dynamic-slice_fusion.4
  222.5 0.9 constant_dynamic-slice_fusion.4
  223.5 0.9 constant_dynamic-slice_fusion.4
  224.5 0.9 constant_dynamic-slice_fusion.4
  225.4 0.9 constant_dynamic-slice_fusion.4
  226.4 0.9 constant_dynamic-slice_fusion.4
  227.4 0.9 constant_dynamic-slice_fusion.4
  228.4 0.9 constant_dynamic-slice_fusion.4
  229.4 0.9 constant_dynamic-slice_fusion.4
  230.4 0.9 constant_dynamic-slice_fusion.4
  231.3 0.9 constant_dynamic-slice_fusion.4
  232.3 0.9 constant_dynamic-slice_fusion.4
  233.3 0.9 constant_dynamic-slice_fusion.4
  234.3 0.9 constant_dynamic-slice_fusion.4
  235.3 0.9 constant_dynamic-slice_fusion.4
  236.3 0.9 constant_dynamic-slice_fusion.4
  237.2 0.9 constant_dynamic-slice_fusion.4
  238.2 0.9 constant_dynamic-slice_fusion.4
  239.2 0.9 constant_dynamic-slice_fusion.4
  240.2 0.9 constant_dynamic-slice_fusion.4
  241.2 0.9 constant_dynamic-slice_fusion.4
  242.2 0.9 constant_dynamic-slice_fusion.4
  243.1 0.9 constant_dynamic-slice_fusion.4
  244.1 0.9 constant_dynamic-slice_fusion.4
  245.1 0.9 constant_dynamic-slice_fusion.4
  246.1 0.9 constant_dynamic-slice_fusion.4
  247.1 15.5 %scatter_custom_fusion.2 = f32[4096]{0:T(1024)S(1)} fusion(s32[4096]{0:T(1024)S(1)} %bitcast.42, f32[4096]{0:T(1024)S(1)} %log_add_fusion, f32[]{:T(128)} %constant.134.clone.1), kind=kCustom, calls=%fused_computation.78 | custom fusion | bytes 16388 | tf_op jit(solution)/shard_map/scatter | solution.py:111
  262.6 1.1 gather_fusion.3
  263.8 1.3 select_reduce_fusion.4
  265.1 9.0 %fusion.39 = f32[4096,768]{1,0:T(8,128)} fusion(bf16[128,768]{1,0:T(8,128)(2,1)S(1)} %copy-done, f32[128,4096]{0,1:T(8,128)S(1)} %get-tuple-element.159, f32[4096]{0:T(1024)S(1)} %log_add_fusion, f32[128]{0:T(128)S(1)} %get-tuple-element.156, s32[128]{0:T(128)S(1)} %fusion.38, f32[]{:T(128)} %bitcast.2, s32[4096]{0:T(1024)S(1)} %fusion.19, ...), kind=kOutput, calls=%fused_computation.97 | convolution fusion | flops 811597824 | bytes 14914692 | tf_op jit(solution)/shard_map/dot_general | solution.py:119
  274.8 234.3 %reduce-scatter.2.cloned.1.call-done = f32[128,768]{1,0:T(8,128)} async-done(((f32[4096,768]{1,0:T(8,128)}), f32[128,768]{1,0:T(8,128)}) %reduce-scatter.2.cloned.1.call-update) | async-done | bytes 393232 | tf_op jit(solution)/shard_map/reduce_scatter | solution.py:118
  509.1 1.0 fusion.8
  510.4 0.5 broadcast.420
  510.9 1.8 reduce
  512.7 0.7 reshape.359
  513.5 5.0 all-to-all-start.1
  518.4 10.0 %fusion.7 = bf16[128,768]{1,0:T(8,128)(2,1)} fusion(bf16[4096,768]{1,0:T(8,128)(2,1)} %all-gather.4.cloned.1.call-done, f32[128,4096]{0,1:T(8,128)S(1)} %get-tuple-element.159, f32[4096]{0:T(1024)S(1)} %log_add_fusion, f32[128]{0:T(128)S(1)} %get-tuple-element.156, s32[128]{0:T(128)S(1)} %fusion.38, f32[]{:T(128)} %bitcast.2, s32[4096]{0:T(1024)S(1)} %fusion.19, ...), kind=kOutput, calls=%fused_computation.28 | convolution fusion | flops 811794432 | bytes 8623236 | tf_op jit(solution)/shard_map/dot_general | solution.py:117
  528.4 72.7 %psum.7 = f32[]{:T(128)} all-reduce(f32[]{:T(128)} %get-tuple-element.155), channel_id=1, replica_groups=mesh['lang'=8,'dp'=32] {'dp'}, use_global_device_ids=true, to_apply=%region_12.13 | all-reduce | flops 1 | bytes 8 | tf_op jit(solution)/shard_map/psum | solution.py:114
  602.0 1.2 gather_fusion.2
  (55 shorter events, 1.6 us)
Async XLA Ops:
  7.2 103.9 %copy-start = (bf16[128,768]{1,0:T(8,128)(2,1)S(1)}, bf16[128,768]{1,0:T(8,128)(2,1)}, u32[]{:S(2)}) copy-start(bf16[128,768]{1,0:T(8,128)(2,1)} %param.8) | copy-start | bytes 589828
  7.2 103.9 %all-gather.4.cloned.1.call-start = ((), (), s32[]{:S(2)}) async-start(), calls=%async_computation.3 | async-start | bytes 6488064 | tf_op jit(solution)/shard_map/all_gather | solution.py:102
  20.8 488.3 %reduce-scatter.2.cloned.1.call-start = ((), (), s32[]{:S(2)}) async-start(), calls=%async_computation.4 | async-start | bytes 12976128 | tf_op jit(solution)/shard_map/reduce_scatter | solution.py:118
  513.5 88.3 %all-to-all-start.1 = ((bf16[8,2,6144]{2,1,0:T(2,128)(2,1)}), bf16[8,2,6144]{2,1,0:T(2,128)(2,1)S(1)}, u32[]{:S(2)}, u32[]{:S(2)}) async-start(bf16[8,2,6144]{2,1,0:T(2,128)(2,1)} %reshape.359), calls=%async_computation.2 | async-start | bytes 393216 | tf_op jit(solution)/shard_map/all_to_all | solution.py:128
Sparse Core Ops, SparseCore 0:
  20.9 90.1 all-gather.3
  274.2 234.7 reduce-scatter.1
where the time goes:
time: 612 us; the launch traced here: 611 us
  waiting for transfers between devices  280 us (46%)
  blocking collectives  179 us (29%)
  local copies, waits for them, and re-layouts  93.5 us (15%)
  matrix products  23.9 us (4%)
  between operations  16.7 us (3%)
  other arithmetic  12.5 us (2%)
    reduce_scatter x1, waiting for transfers between devices, per_device(): lax.psum_scatter(lax.dot_general(grad_tile, src_emb, (((0,), (0,)), ((),...  234 us
    all_gather x2, blocking collectives, combined_all(): everything = jax.tree.map(lambda part: lax.all_gather(part, axis), value)  95.5 us
    psum x1, blocking collectives, per_device(): loss_total = lax.psum(jnp.sum(terms), 'dp')  72.7 us
    all_gather x1, waiting for transfers between devices, per_device(): all_targets = lax.all_gather(partner, 'dp', axis=0, tiled=True)  45.6 us
    dynamic_slice x31, local copies, waits for them, and re-layouts, lap(): return combine(so_far, jax.tree.map(lambda part: part[k], everything))  29 us
    gather x1, local copies, waits for them, and re-layouts, tile_scores(): col_ok = col_live_global[tgt_index] > 0.5  23 us
    scatter x1, local copies, waits for them, and re-layouts, per_device(): jnp.zeros((pair_rows,), jnp.float32).at[gathered_index].set(col_lse_all)  15.5 us
    scatter x1, local copies, waits for them, and re-layouts, per_device(): col_live_global = jnp.zeros((pair_rows,), jnp.float32).at[pair_align].set...  15.5 us
  transfers between devices with their start and end apart: 3, of which 2 were waited for; matrix products, arithmetic and copies ran while one was open for 9% of the time, Pallas kernels for 0%

commit v1 on v0

--- a/solution.py
+++ b/solution.py
@@ -99,7 +99,9 @@
     gathered_index = target_index(0, pair_rows, row_count, per_slot, data_size)
     col_live_gathered = col_live_global[gathered_index]
     start_max = jnp.full((row_count,), LOW_FILL, jnp.float32)
-    all_targets = lax.all_gather(partner, "dp", axis=0, tiled=True)
+    all_targets = jnp.concatenate(
+        lax.all_to_all(jnp.stack([partner] * lax.axis_size("dp")), "dp", 0, 0), axis=0
+    )
     scores_f, is_pos, col_ok = tile_scores(
         src_emb, all_targets, 0, my_align, col_live_global, per_slot, data_size, inv_root
     )

time: 612 us -> 682 us (1.11)
  waiting for transfers between devices: 280 us -> 332 us
  starting transfers between devices: 5.06 us -> 16.5 us
    all_to_all x0 -> x1, waiting for transfers between devices: none -> 96.6 us  [per_device(): lax.all_to_all(jnp.stack([partner] * lax.axis_size('dp')), 'dp', 0, 0)]
    all_gather x1 -> x0, waiting for transfers between devices: 45.6 us -> none  [per_device(): all_targets = lax.all_gather(partner, 'dp', axis=0, tiled=True)]
    all_to_all x0 -> x1, starting transfers between devices: none -> 11.7 us  [per_device(): lax.all_to_all(jnp.stack([partner] * lax.axis_size('dp')), 'dp', 0, 0)]
  transfers between devices with their start and end apart: 3 -> 3, of which waited for: 2 -> 2; matrix products, arithmetic and copies ran while one was open for 9% -> 8% of each run, Pallas kernels for 0% -> 0%
where the time goes in v1:
time: 682 us; the launch traced here: 680 us
  waiting for transfers between devices  332 us (49%)
  blocking collectives  185 us (27%)
  local copies, waits for them, and re-layouts  94.9 us (14%)
  matrix products  23.9 us (4%)
  between operations  16.7 us (2%)
  starting transfers between devices  16.5 us (2%)
  other arithmetic  11.1 us (2%)
    reduce_scatter x1, waiting for transfers between devices, per_device(): lax.psum_scatter(lax.dot_general(grad_tile, src_emb, (((0,), (0,)), ((),...  235 us
    all_gather x2, blocking collectives, combined_all(): everything = jax.tree.map(lambda part: lax.all_gather(part, axis), value)  102 us
    all_to_all x1, waiting for transfers between devices, per_device(): lax.all_to_all(jnp.stack([partner] * lax.axis_size('dp')), 'dp', 0, 0)  96.6 us
    psum x1, blocking collectives, per_device(): loss_total = lax.psum(jnp.sum(terms), 'dp')  72.7 us
    dynamic_slice x31, local copies, waits for them, and re-layouts, lap(): return combine(so_far, jax.tree.map(lambda part: part[k], everything))  29 us
    gather x1, local copies, waits for them, and re-layouts, tile_scores(): col_ok = col_live_global[tgt_index] > 0.5  23 us
    scatter x1, local copies, waits for them, and re-layouts, per_device(): jnp.zeros((pair_rows,), jnp.float32).at[gathered_index].set(col_lse_all)  15.5 us
    scatter x1, local copies, waits for them, and re-layouts, per_device(): col_live_global = jnp.zeros((pair_rows,), jnp.float32).at[pair_align].set...  15.5 us
  transfers between devices with their start and end apart: 3, of which 2 were waited for; matrix products, arithmetic and copies ran while one was open for 8% of the time, Pallas kernels for 0%

profile of v1, /device:TPU:2, one launch (start us, length us, event | category | flops | bytes accessed | tf_op | source)
XLA Modules:
  0.0 680.3 jit_solution(5210258846228634929)
XLA Ops:
  7.2 0.7 compare_select_fusion.9
  7.9 0.6 scatter_custom_fusion.1
  8.5 1.5 gather_fusion.1
  10.0 10.0 %all_to_all.29 = bf16[8,16,768]{2,1,0:T(8,128)(2,1)S(1)} all-to-all(bf16[8,16,768]{2,1,0:T(8,128)(2,1)S(1)} %gather_fusion.1), channel_id=1, replica_groups=mesh['lang'=8,'dp'=32] {'lang'}, dimensions={0} | all-to-all | bytes 393216 | tf_op jit(solution)/shard_map/all_to_all | solution.py:85
  20.1 3.4 stack.3
  23.4 11.7 %all-to-all-start.1 = ((bf16[32,128,768]{2,1,0:T(8,128)(2,1)}), bf16[32,128,768]{2,1,0:T(8,128)(2,1)}, u32[]{:S(2)}, u32[]{:S(2)}) async-start(bf16[32,128,768]{2,1,0:T(8,128)(2,1)} %stack.3), calls=%async_computation.1 | async-start | bytes 12582912 | tf_op jit(solution)/shard_map/all_to_all | solution.py:103
  35.2 0.6 dynamic_slice.32
  35.8 0.7 dynamic_slice.31
  36.5 0.6 fusion.29
  37.1 15.5 %scatter_custom_fusion = f32[4096]{0:T(1024)S(1)} fusion(s32[4096]{0:T(1024)S(1)} %bitcast.44, f32[4096]{0:T(1024)S(1)} %fusion.29, f32[]{:T(128)} %constant.134.clone.1), kind=kCustom, calls=%fused_computation.80 | custom fusion | bytes 16388 | tf_op jit(solution)/shard_map/scatter | solution.py:94
  52.8 23.0 %gather_fusion = f32[4096]{0:T(1024)S(1)} fusion(f32[4096]{0:T(1024)S(1)} %scatter_custom_fusion, s32[4096]{0:T(1024)S(1)} %broadcast_clamp_fusion), kind=kCustom, calls=%fused_computation | custom fusion | bytes 49152 | tf_op jit(solution)/shard_map/gather | solution.py:38
  75.8 0.7 add_compare_fusion
  76.6 96.6 %all-to-all-done.1 = bf16[32,128,768]{2,1,0:T(8,128)(2,1)} async-done(((bf16[32,128,768]{2,1,0:T(8,128)(2,1)}), bf16[32,128,768]{2,1,0:T(8,128)(2,1)}, u32[]{:S(2)}, u32[]{:S(2)}) %all-to-all-start.1) | async-done | bytes 6291488 | tf_op jit(solution)/shard_map/all_to_all | solution.py:103
  173.1 4.9 select_reduce_fusion.3
  178.1 53.1 %all-gather = f32[131072]{0:T(1024)S(1)} all-gather(f32[4096]{0:T(1024)S(1)} %get-tuple-element.142), channel_id=2, replica_groups=mesh['lang'=8,'dp'=32] {'dp'}, dimensions={0}, use_global_device_ids=true | all-gather | bytes 540672 | tf_op jit(solution)/shard_map/all_gather | solution.py:12
  231.3 4.1 fusion.6
  235.4 48.8 %all-gather.1 = f32[131072]{0:T(1024)S(1)} all-gather(f32[4096]{0:T(1024)S(1)} %get-tuple-element.139), channel_id=3, replica_groups=mesh['lang'=8,'dp'=32] {'dp'}, dimensions={0}, use_global_device_ids=true | all-gather | bytes 540672 | tf_op jit(solution)/shard_map/all_gather | solution.py:12
  284.2 0.9 reshape.350
  285.1 30.4 %while.17 = (s32[]{:T(128)}, f32[4096]{0:T(1024)S(1)}, f32[4096]{0:T(1024)S(1)}, f32[32,4096]{1,0:T(8,128)S(1)}, f32[32,4096]{1,0:T(8,128)}, /*index=5*/s32[]{:T(128)}, s32[]{:T(128)}, s32[]{:T(128)}) while((s32[]{:T(128)}, f32[4096]{0:T(1024)S(1)}, f32[4096]{0:T(1024)S(1)}, f32[32,4096]{1,0:T(8,128)S(1)}, f32[32,4096]{1,0:T(8,128)}, ...), condition=%wide.region_7.8_spmd, body=%wide.region_6.7_spmd.sunk | while | flops 24581 | bytes 163971 | solution.py:18
  285.1 0.9 constant_dynamic-slice_fusion.4
  286.0 0.9 constant_dynamic-slice_fusion.4
  287.0 0.9 constant_dynamic-slice_fusion.4
  288.0 0.9 constant_dynamic-slice_fusion.4
  289.0 0.9 constant_dynamic-slice_fusion.4
  290.0 0.9 constant_dynamic-slice_fusion.4
  290.9 0.9 constant_dynamic-slice_fusion.4
  291.9 0.9 constant_dynamic-slice_fusion.4
  292.9 0.9 constant_dynamic-slice_fusion.4
  293.9 0.9 constant_dynamic-slice_fusion.4
  294.9 0.9 constant_dynamic-slice_fusion.4
  295.9 0.9 constant_dynamic-slice_fusion.4
  296.8 0.9 constant_dynamic-slice_fusion.4
  297.8 0.9 constant_dynamic-slice_fusion.4
  298.8 0.9 constant_dynamic-slice_fusion.4
  299.8 0.9 constant_dynamic-slice_fusion.4
  300.8 0.9 constant_dynamic-slice_fusion.4
  301.8 0.9 constant_dynamic-slice_fusion.4
  302.7 0.9 constant_dynamic-slice_fusion.4
  303.7 0.9 constant_dynamic-slice_fusion.4
  304.7 0.9 constant_dynamic-slice_fusion.4
  305.7 0.9 constant_dynamic-slice_fusion.4
  306.7 0.9 constant_dynamic-slice_fusion.4
  307.6 0.9 constant_dynamic-slice_fusion.4
  308.6 0.9 constant_dynamic-slice_fusion.4
  309.6 0.9 constant_dynamic-slice_fusion.4
  310.6 0.9 constant_dynamic-slice_fusion.4
  311.6 0.9 constant_dynamic-slice_fusion.4
  312.6 0.9 constant_dynamic-slice_fusion.4
  313.5 0.9 constant_dynamic-slice_fusion.4
  314.5 0.9 constant_dynamic-slice_fusion.4
  315.5 15.5 %scatter_custom_fusion.2 = f32[4096]{0:T(1024)S(1)} fusion(s32[4096]{0:T(1024)S(1)} %bitcast.43, f32[4096]{0:T(1024)S(1)} %log_add_fusion, f32[]{:T(128)} %constant.134.clone.1), kind=kCustom, calls=%fused_computation.78 | custom fusion | bytes 16388 | tf_op jit(solution)/shard_map/scatter | solution.py:113
  331.1 1.1 gather_fusion.3
  332.2 1.3 select_reduce_fusion.4
  333.5 9.0 %fusion.39 = f32[4096,768]{1,0:T(8,128)} fusion(bf16[128,768]{1,0:T(8,128)(2,1)S(1)} %copy-done, f32[128,4096]{0,1:T(8,128)S(1)} %get-tuple-element.159, f32[4096]{0:T(1024)S(1)} %log_add_fusion, f32[128]{0:T(128)S(1)} %get-tuple-element.156, s32[128]{0:T(128)S(1)} %fusion.38, f32[]{:T(128)} %bitcast.2, s32[4096]{0:T(1024)S(1)} %fusion.19, ...), kind=kOutput, calls=%fused_computation.97 | convolution fusion | flops 811597824 | bytes 14914692 | tf_op jit(solution)/shard_map/dot_general | solution.py:121
  343.2 235.2 %reduce-scatter.2.cloned.1.call-done = f32[128,768]{1,0:T(8,128)} async-done(((f32[4096,768]{1,0:T(8,128)}), f32[128,768]{1,0:T(8,128)}) %reduce-scatter.2.cloned.1.call-update) | async-done | bytes 393232 | tf_op jit(solution)/shard_map/reduce_scatter | solution.py:120
  578.4 1.0 fusion.8
  579.4 0.3 copy.13
  579.7 0.5 broadcast.421
  580.2 1.8 reduce
  582.1 0.7 reshape.364
  582.8 4.8 all-to-all-start.2
  587.6 10.0 %fusion.7 = bf16[128,768]{1,0:T(8,128)(2,1)} fusion(bf16[4096,768]{1,0:T(8,128)(2,1)} %bitcast.8, f32[128,4096]{0,1:T(8,128)S(1)} %get-tuple-element.159, f32[4096]{0:T(1024)S(1)} %log_add_fusion, f32[128]{0:T(128)S(1)} %get-tuple-element.156, s32[128]{0:T(128)S(1)} %fusion.38, f32[]{:T(128)} %bitcast.2, s32[4096]{0:T(1024)S(1)} %fusion.19, ...), kind=kOutput, calls=%fused_computation.28 | convolution fusion | flops 811794432 | bytes 8623236 | tf_op jit(solution)/shard_map/dot_general | solution.py:119
  597.5 72.7 %psum.7 = f32[]{:T(128)} all-reduce(f32[]{:T(128)} %get-tuple-element.155), channel_id=1, replica_groups=mesh['lang'=8,'dp'=32] {'dp'}, use_global_device_ids=true, to_apply=%region_12.13 | all-reduce | flops 1 | bytes 8 | tf_op jit(solution)/shard_map/psum | solution.py:116
  671.1 1.2 gather_fusion.2
  (61 shorter events, 1.3 us)
Async XLA Ops:
  7.2 166.0 %copy-start = (bf16[128,768]{1,0:T(8,128)(2,1)S(1)}, bf16[128,768]{1,0:T(8,128)(2,1)}, u32[]{:S(2)}) copy-start(bf16[128,768]{1,0:T(8,128)(2,1)} %param.8) | copy-start | bytes 589828
  23.4 11.8 %copy-start.2 = (s32[8]{0:T(128)S(1)}, s32[8]{0:T(128)}, u32[]{:S(2)}) copy-start(s32[8]{0:T(128)} %param.11) | copy-start | bytes 100
  23.4 12.4 %copy-start.3 = (f32[8]{0:T(128)S(1)}, f32[8]{0:T(128)}, u32[]{:S(2)}) copy-start(f32[8]{0:T(128)} %param.13) | copy-start | bytes 100
  23.4 13.7 %copy-start.1 = (s32[1,4096]{1,0:T(1,128)S(1)}, s32[1,4096]{1,0:T(1,128)}, u32[]{:S(2)}) copy-start(s32[1,4096]{1,0:T(1,128)} %param.12) | copy-start | bytes 49156
  23.4 149.7 %all-to-all-start.1 = ((bf16[32,128,768]{2,1,0:T(8,128)(2,1)}), bf16[32,128,768]{2,1,0:T(8,128)(2,1)}, u32[]{:S(2)}, u32[]{:S(2)}) async-start(bf16[32,128,768]{2,1,0:T(8,128)(2,1)} %stack.3), calls=%async_computation.1 | async-start | bytes 12582912 | tf_op jit(solution)/shard_map/all_to_all | solution.py:103
  35.1 543.3 %reduce-scatter.2.cloned.1.call-start = ((), (), s32[]{:S(2)}) async-start(), calls=%async_computation.4 | async-start | bytes 12976128 | tf_op jit(solution)/shard_map/reduce_scatter | solution.py:120
  582.8 88.1 %all-to-all-start.2 = ((bf16[8,2,6144]{2,1,0:T(2,128)(2,1)}), bf16[8,2,6144]{2,1,0:T(2,128)(2,1)S(1)}, u32[]{:S(2)}, u32[]{:S(2)}) async-start(bf16[8,2,6144]{2,1,0:T(2,128)(2,1)} %reshape.364), calls=%async_computation.3 | async-start | bytes 393216 | tf_op jit(solution)/shard_map/all_to_all | solution.py:130
Sparse Core Ops, SparseCore 0:
  342.7 235.6 reduce-scatter.1
